TPU v7x, 32 devices: a whole 2x2x4 slice. The times are simulated.
32 devices in a mesh: dp: 2 (over core), section: 4 (over y, x), expert: 4 (over z).
Axes of the slice: x: 2, y: 2, z: 4, core: 2. Of those that a mesh axis runs over, the one named last changes fastest.
Arguments:
- grad_out: bfloat16 [1024, 3584], P(('dp', 'expert'), 'section'), may hold values from -6 to 6
- expert_ids: int32 [1024, 8], P(('dp', 'expert')), may hold values from 0 to 63, all different within a row; in each aligned block of 128 rows (0 to 127, 128 to 255, ...) at most 24 rows name the same one
- gate_weights: float32 [1024, 8], P(('dp', 'expert')), may hold values from 0.1 to 1
- act: bfloat16 [1024, 8, 1024], P(('dp', 'expert'), None, 'section'), may hold values from -0.8984375 to 0.8984375
- w_down: bfloat16 [64, 1024, 3584], P('expert', 'section'), may hold values from -0.09375 to 0.09375
Outputs:
- grad_hidden: bfloat16 [1024, 8, 1024], P(('dp', 'expert'), None, 'section')
- grad_gates: float32 [1024, 8], P(('dp', 'expert'))
- grad_w: bfloat16 [64, 1024, 3584], P('expert', 'section', 'dp')
Inputs may be any that keep to these rules, and one draw needn't show every extreme that they name: `expert_ids`: each row names 8 different experts. In each aligned block of 128 rows (the tokens of one device) no expert is named by more than 24 rows, and in every draw some expert is named by exactly 24 rows of some block.
All inputs are finite; a program needn't handle non-finite values.
Results may differ from a plain program's by a relative error of at most 0.0058.
Values may be sent and summed in bfloat16 or wider, within the bound.
A program may use at most 128 MiB of HBM per device.

v0:
```python
import jax
import jax.numpy as jnp
from jax import lax
from jax.sharding import PartitionSpec as P


def arrange(received, n_expert, exp_dev):
    capacity = received.shape[1]
    width = received.shape[2]
    grouped = received.reshape(n_expert, exp_dev, capacity, width)
    return jnp.transpose(grouped, (1, 0, 2, 3)).reshape(exp_dev, n_expert * capacity, width)


def local(grad_out, expert_ids, gate_weights, act, w_down):
    tok_count, top_count = expert_ids.shape
    hidden_slice = act.shape[2]
    exp_dev = w_down.shape[0]
    n_expert = lax.axis_size("expert")
    experts = exp_dev * n_expert
    capacity = 3 * tok_count * top_count // (2 * experts)
    pair_count = tok_count * top_count
    targets = expert_ids.reshape(pair_count)
    onehot = (targets[:, None] == jnp.arange(experts, dtype=jnp.int32)[None, :]).astype(jnp.int32)
    order_in = jnp.sum((jnp.cumsum(onehot, axis=0) - onehot) * onehot, axis=1)
    position = targets * capacity + order_in
    source = (
        jnp.full((experts * capacity,), pair_count, jnp.int32)
        .at[position]
        .set(jnp.arange(pair_count, dtype=jnp.int32))
    )
    filled = source < pair_count
    token_index = jnp.where(filled, source // top_count, tok_count)
    scaled = (
        (gate_weights[:, :, None] * act.astype(jnp.float32))
        .astype(jnp.bfloat16)
        .reshape(pair_count, hidden_slice)
    )
    scaled_ext = jnp.concatenate([scaled, jnp.zeros((1, hidden_slice), jnp.bfloat16)], axis=0)
    send_scaled = scaled_ext[jnp.where(filled, source, pair_count)].reshape(
        experts, capacity, hidden_slice
    )
    full_rows = lax.all_gather(grad_out, "section", axis=1, tiled=True)
    rows_ext = jnp.concatenate(
        [full_rows, jnp.zeros((1, full_rows.shape[1]), jnp.bfloat16)], axis=0
    )
    send_grad = rows_ext[token_index].reshape(experts, capacity, full_rows.shape[1])
    recv_grad, recv_scaled = (
        lax.all_to_all(send_grad, "expert", split_axis=0, concat_axis=0, tiled=True),
        lax.all_to_all(send_scaled, "expert", split_axis=0, concat_axis=0, tiled=True),
    )
    recv_grad = arrange(recv_grad, n_expert, exp_dev)
    recv_scaled = arrange(recv_scaled, n_expert, exp_dev)
    unscaled = jnp.einsum("erd,ehd->erh", recv_grad, w_down, preferred_element_type=jnp.float32)
    weight_part = jnp.einsum(
        "erh,erd->ehd", recv_scaled, recv_grad, preferred_element_type=jnp.float32
    )
    grad_w = lax.psum_scatter(
        weight_part.astype(jnp.bfloat16), "dp", scatter_dimension=2, tiled=True
    )
    returning = unscaled.astype(jnp.bfloat16).reshape(exp_dev, n_expert, capacity, hidden_slice)
    returning = jnp.transpose(returning, (1, 0, 2, 3)).reshape(experts, capacity, hidden_slice)
    returned = lax.all_to_all(returning, "expert", split_axis=0, concat_axis=0, tiled=True)
    unscaled_tok = returned.reshape(experts * capacity, hidden_slice)[position].reshape(
        tok_count, top_count, hidden_slice
    )
    grad_hidden = (gate_weights[:, :, None] * unscaled_tok.astype(jnp.float32)).astype(jnp.bfloat16)
    gate_share = jnp.sum(act.astype(jnp.float32) * unscaled_tok.astype(jnp.float32), axis=2)
    grad_gates = lax.psum(gate_share, "section")
    return (grad_hidden, grad_gates, grad_w)


def solution(mesh):
    placed = (
        P(("dp", "expert"), "section"),
        P(("dp", "expert"), None),
        P(("dp", "expert"), None),
        P(("dp", "expert"), None, "section"),
        P("expert", "section", None),
    )
    return jax.shard_map(
        local,
        mesh=mesh,
        in_specs=placed,
        out_specs=(
            P(("dp", "expert"), None, "section"),
            P(("dp", "expert"), None),
            P("expert", "section", "dp"),
        ),
        check_vma=False,
    )
```

profile of v0, /device:TPU:0, one launch (start us, length us, event | category | flops | bytes accessed | tf_op | source)
XLA Modules:
  0.0 439.6 jit_solution(6114744383937227593)
XLA Ops:
  7.2 0.7 broadcast_multiply_fusion
  7.9 0.8 copy.20
  9.1 18.0 %reduce-window.6 = s32[64,8,128]{2,1,0:T(8,128)S(1)} reduce-window(s32[64,8,128]{2,1,0:T(8,128)S(1)} %fusion.7, s32[]{:T(128)} %constant.16.clone.1), window={size=1x1x128 pad=0_0x0_0x127_0}, to_apply=%region_0.0 | reduce-window | flops 8323072 | bytes 524292 | tf_op jit(solution)/shard_map/reduce-window
  27.1 0.1 slice.14
  27.2 0.1 copy.22
  27.5 0.1 broadcast_add_fusion
  27.7 4.3 scatter_custom_fusion
  32.1 15.9 %all_gather.3 = bf16[128,3584]{1,0:T(8,128)(2,1)S(1)} all-gather(bf16[128,896]{1,0:T(8,128)(2,1)} %param.5), channel_id=1, replica_groups=mesh['dp'=2,'section'=4,'expert'=4] {'section'}, dimensions={1}, use_global_device_ids=true | all-gather | bytes 1146880 | tf_op jit(solution)/shard_map/all_gather | solution.py:42
  48.1 9.0 %gather_fusion = bf16[1536,3584]{1,0:T(8,128)(2,1)} fusion(bf16[129,3584]{1,0:T(8,128)(2,1)S(1)} %concatenate.6, s32[2048]{0:T(1024)S(1)} %pad_clamp_fusion.1), kind=kCustom, calls=%fused_computation | custom fusion | bytes 22026240 | tf_op jit(solution)/shard_map/gather | solution.py:46
  57.1 242.9 %all_to_all.15 = bf16[64,24,3584]{2,1,0:T(8,128)(2,1)S(1)} all-to-all(bf16[64,24,3584]{2,1,0:T(8,128)(2,1)} %bitcast.48), channel_id=1, replica_groups=mesh['dp'=2,'section'=4,'expert'=4] {'expert'}, dimensions={0} | all-to-all | bytes 22020096 | tf_op jit(solution)/shard_map/all_to_all | solution.py:48
  299.9 4.8 %copy.24 = bf16[16,4,24,3584]{3,2,1,0:T(8,128)(2,1)} copy(bf16[16,4,24,3584]{3,2,0,1:T(8,128)(2,1)S(1)} %bitcast.49) | data formatting | bytes 22020096 | tf_op jit(solution)/shard_map/transpose | solution.py:11
  304.7 16.4 %convolution_convert_fusion.1 = bf16[16,96,256]{2,1,0:T(8,128)(2,1)S(1)} fusion(bf16[16,96,3584]{2,1,0:T(8,128)(2,1)} %bitcast.46, bf16[16,256,3584]{2,1,0:T(8,128)(2,1)} %param.9), kind=kOutput, calls=%fused_computation.5 | convolution fusion | flops 2818965504 | bytes 41156608 | tf_op jit(solution)/shard_map/erd,ehd->erh/dot_general | solution.py:53
  321.1 0.9 copy.25
  322.0 3.5 all-to-all-start.1
  325.6 0.1 copy.18
  325.7 18.8 %all-to-all-done.1 = bf16[64,24,256]{2,1,0:T(8,128)(2,1)S(1)} async-done(((bf16[64,24,256]{2,1,0:T(8,128)(2,1)}), bf16[64,24,256]{2,1,0:T(8,128)(2,1)S(1)}, u32[]{:S(2)}, u32[]{:S(2)}) %all-to-all-start.1) | async-done | bytes 786464 | tf_op jit(solution)/shard_map/all_to_all | solution.py:62
  344.5 3.9 gather_fusion.1
  348.5 1.2 fusion.3
  349.7 4.8 %gather_fusion.2 = bf16[1536,256]{1,0:T(8,128)(2,1)S(1)} fusion(bf16[1025,256]{1,0:T(8,128)(2,1)S(1)} %concatenate.7, s32[2048]{0:T(1024)S(1)} %pad_clamp_fusion), kind=kCustom, calls=%fused_computation.2 | custom fusion | bytes 1579008 | tf_op jit(solution)/shard_map/gather | solution.py:39
  354.5 22.1 %all_to_all.16 = bf16[64,24,256]{2,1,0:T(8,128)(2,1)S(1)} all-to-all(bf16[64,24,256]{2,1,0:T(8,128)(2,1)S(1)} %bitcast.54), channel_id=1, replica_groups=mesh['dp'=2,'section'=4,'expert'=4] {'expert'}, dimensions={0} | all-to-all | bytes 1572864 | tf_op jit(solution)/shard_map/all_to_all | solution.py:49
  376.6 18.5 %convolution_convert_fusion = bf16[16,256,3584]{2,1,0:T(8,128)(2,1)} fusion(bf16[16,96,256]{2,1,0:T(8,128)(2,1)S(1)} %bitcast.52, bf16[16,96,3584]{2,1,0:T(8,128)(2,1)} %bitcast.47), kind=kOutput, calls=%fused_computation.4 | convolution fusion | flops 2833252352 | bytes 41156608 | tf_op jit(solution)/shard_map/erh,erd->ehd/dot_general | solution.py:54
  395.1 15.1 %psum.7 = f32[128,8]{1,0:T(8,128)S(1)} all-reduce(f32[128,8]{1,0:T(8,128)S(1)} %get-tuple-element.7), channel_id=1, replica_groups=mesh['dp'=2,'section'=4,'expert'=4] {'section'}, use_global_device_ids=true, to_apply=%region_5.6 | all-reduce | flops 1024 | bytes 8192 | tf_op jit(solution)/shard_map/psum | solution.py:68
  410.3 0.7 copy.27
  411.0 21.8 %reduce-scatter.2.cloned.1.call-done = bf16[16,256,1792]{2,1,0:T(8,128)(2,1)} async-done(((bf16[16,256,3584]{2,1,0:T(8,128)(2,1)}), bf16[16,256,1792]{2,1,0:T(8,128)(2,1)}) %reduce-scatter.2.cloned.1.call-update) | async-done | bytes 14680080 | tf_op jit(solution)/shard_map/reduce_scatter | solution.py:57
  (24 shorter events, 0.9 us)
Async XLA Ops:
  304.7 20.8 %copy-start.1 = (f32[128,8]{0,1:T(8,128)S(1)}, f32[128,8]{0,1:T(8,128)}, u32[]{:S(2)}) copy-start(f32[128,8]{0,1:T(8,128)} %param.7) | copy-start | bytes 12292
  304.7 43.8 %copy-start = (bf16[128,8,256]{2,1,0:T(8,128)(2,1)S(1)}, bf16[128,8,256]{2,1,0:T(8,128)(2,1)}, u32[]{:S(2)}) copy-start(bf16[128,8,256]{2,1,0:T(8,128)(2,1)} %param.8) | copy-start | bytes 1572868
  322.0 22.5 %all-to-all-start.1 = ((bf16[64,24,256]{2,1,0:T(8,128)(2,1)}), bf16[64,24,256]{2,1,0:T(8,128)(2,1)S(1)}, u32[]{:S(2)}, u32[]{:S(2)}) async-start(bf16[64,24,256]{2,1,0:T(8,128)(2,1)} %bitcast.10), calls=%async_computation.1 | async-start | bytes 1572864 | tf_op jit(solution)/shard_map/all_to_all | solution.py:62
  325.5 107.2 %reduce-scatter.2.cloned.1.call-start = ((), (), s32[]{:S(2)}) async-start(), calls=%async_computation.4 | async-start | bytes 44040192 | tf_op jit(solution)/shard_map/reduce_scatter | solution.py:57
Sparse Core Ops, SparseCore 0:
  395.3 37.4 reduce-scatter.1
where the time goes:
time: 440 us
  blocking collectives  296 us (67%)
  waiting for transfers between devices  40.6 us (9%)
  matrix products  34.9 us (8%)
  local copies, waits for them, and re-layouts  30.2 us (7%)
  other arithmetic  20.2 us (5%)
  between operations  14.2 us (3%)
    all_to_all x1, blocking collectives, local(): lax.all_to_all(send_grad, 'expert', split_axis=0, concat_axis=0, tiled=True)  243 us
    all_to_all x1, blocking collectives, local(): lax.all_to_all(send_scaled, 'expert', split_axis=0, concat_axis=0, tiled=...  22.1 us
    reduce_scatter x1, waiting for transfers between devices, local(): lax.psum_scatter(weight_part.astype(jnp.bfloat16), 'dp', scatter_dimensio...  21.8 us
    all_to_all x1, waiting for transfers between devices, local(): lax.all_to_all(returning, 'expert', split_axis=0, concat_axis=0, tiled=True)  18.8 us
    dot_general x1, matrix products, local(): jnp.einsum('erh,erd->ehd', recv_scaled, recv_grad, preferred_element_type...  18.5 us
    another operation x3, other arithmetic  18.2 us
    dot_general x1, matrix products, local(): jnp.einsum('erd,ehd->erh', recv_grad, w_down, preferred_element_type=jnp....  16.4 us
    all_gather x1, blocking collectives, local(): full_rows = lax.all_gather(grad_out, 'section', axis=1, tiled=True)  15.9 us
  transfers between devices with their start and end apart: 2, of which 2 were waited for; matrix products, arithmetic and copies ran while one was open for 0% of the time, Pallas kernels for 0%

commit v1 on v0

v1 whole, which is shorter than its diff:
```python
import functools

import jax
import jax.numpy as jnp
from jax import lax
from jax.experimental import pallas as pl
from jax.experimental.pallas import tpu as pltpu
from jax.sharding import PartitionSpec as P

BF = jnp.bfloat16
F32 = jnp.float32
MESH = pl.DeviceIdType.MESH


def slots_of(expert_ids, experts, capacity):
    tok_count = expert_ids.shape[0]
    onehot = expert_ids[:, :, None] == jnp.arange(experts, dtype=jnp.int32)
    named = jnp.any(onehot, axis=1).astype(BF)
    earlier = jnp.arange(tok_count)[:, None] > jnp.arange(tok_count)[None, :]
    before = jnp.dot(earlier.astype(BF), named, preferred_element_type=F32)
    order_in = jnp.sum(jnp.where(onehot, before[:, None, :], 0.0), axis=2).astype(jnp.int32)
    return expert_ids * capacity + order_in


def arrange(received, n_expert, exp_dev):
    capacity = received.shape[1]
    width = received.shape[2]
    grouped = received.reshape(n_expert, exp_dev, capacity, width)
    return jnp.transpose(grouped, (1, 0, 2, 3)).reshape(exp_dev, n_expert * capacity, width)


def local_general(grad_out, expert_ids, gate_weights, act, w_down):
    tok_count, top_count = expert_ids.shape
    hidden_slice = act.shape[2]
    exp_dev = w_down.shape[0]
    n_expert = lax.axis_size("expert")
    experts = exp_dev * n_expert
    capacity = 3 * tok_count * top_count // (2 * experts)
    pair_count = tok_count * top_count
    position = slots_of(expert_ids, experts, capacity).reshape(pair_count)
    source = (
        jnp.full((experts * capacity,), pair_count, jnp.int32)
        .at[position]
        .set(jnp.arange(pair_count, dtype=jnp.int32))
    )
    filled = source < pair_count
    token_index = jnp.where(filled, source // top_count, tok_count)
    scaled = (
        (gate_weights[:, :, None] * act.astype(F32)).astype(BF).reshape(pair_count, hidden_slice)
    )
    scaled_ext = jnp.concatenate([scaled, jnp.zeros((1, hidden_slice), BF)], axis=0)
    send_scaled = scaled_ext[jnp.where(filled, source, pair_count)].reshape(
        experts, capacity, hidden_slice
    )
    full_rows = lax.all_gather(grad_out, "section", axis=1, tiled=True)
    rows_ext = jnp.concatenate([full_rows, jnp.zeros((1, full_rows.shape[1]), BF)], axis=0)
    send_grad = rows_ext[token_index].reshape(experts, capacity, full_rows.shape[1])
    recv_grad, recv_scaled = (
        lax.all_to_all(send_grad, "expert", split_axis=0, concat_axis=0, tiled=True),
        lax.all_to_all(send_scaled, "expert", split_axis=0, concat_axis=0, tiled=True),
    )
    recv_grad = arrange(recv_grad, n_expert, exp_dev)
    recv_scaled = arrange(recv_scaled, n_expert, exp_dev)
    unscaled = jnp.einsum("erd,ehd->erh", recv_grad, w_down, preferred_element_type=F32)
    weight_part = jnp.einsum("erh,erd->ehd", recv_scaled, recv_grad, preferred_element_type=F32)
    grad_w = lax.psum_scatter(weight_part.astype(BF), "dp", scatter_dimension=2, tiled=True)
    returning = unscaled.astype(BF).reshape(exp_dev, n_expert, capacity, hidden_slice)
    returning = jnp.transpose(returning, (1, 0, 2, 3)).reshape(experts, capacity, hidden_slice)
    returned = lax.all_to_all(returning, "expert", split_axis=0, concat_axis=0, tiled=True)
    unscaled_tok = returned.reshape(experts * capacity, hidden_slice)[position].reshape(
        tok_count, top_count, hidden_slice
    )
    grad_hidden = (gate_weights[:, :, None] * unscaled_tok.astype(F32)).astype(BF)
    gate_share = jnp.sum(act.astype(F32) * unscaled_tok.astype(F32), axis=2)
    return (grad_hidden, lax.psum(gate_share, "section"), grad_w)


def spread(
    g_ref, ids_ref, s_ref, g_all, g_half, ids_all, s_all, here,
    a_snd, a_rcv, x_snd, x_rcv, y_snd, y_rcv, d_snd, d_rcv, h_snd, h_rcv,
    s_snd, s_rcv, f_snd, f_rcv, i_snd, i_rcv,
):
    dp, sec, z = (lax.axis_index(a) for a in ("dp", "section", "expert"))
    width = g_ref.shape[1]
    half = g_half.shape[2]
    mate = 1 - dp
    sx = sec + 1 - 2 * (sec % 2)
    sy = (sec + 2) % 4
    to_mate, to_x, to_y = (mate, sec, z), (dp, sx, z), (dp, sy, z)
    to_z = [(dp, sec, (z + j) % 4) for j in range(4)]
    other = [(mate, sec, (z + j) % 4) for j in range(4)]
    peers = [to_mate, to_x, to_y] + to_z[1:] + other[1:]

    barrier = pltpu.get_barrier_semaphore()
    for peer in peers:
        pl.semaphore_signal(barrier, inc=1, device_id=peer, device_id_type=MESH)
    pl.semaphore_wait(barrier, len(peers))

    def send(src, dst, snd, rcv, to):
        copy = pltpu.make_async_remote_copy(
            src_ref=src, dst_ref=dst, send_sem=snd, recv_sem=rcv, device_id=to, device_id_type=MESH
        )
        copy.start()
        return copy

    def cols(s):
        return pl.ds(pl.multiple_of(s * width, 128), width)

    zs = [(z + 4 - j) % 4 for j in range(4)]

    def shard(j, s):
        return g_all.at[zs[j], :, cols(s)]

    order = (1, 3, 2)
    a = {j: send(g_ref, shard(0, sec), a_snd.at[j], a_rcv.at[j], to_z[j]) for j in order}
    x = {0: send(g_ref, shard(0, sec), x_snd.at[0], x_rcv.at[0], to_x)}
    y = {0: send(g_ref, shard(0, sec), y_snd.at[0], y_rcv.at[0], to_y)}
    own = [
        pltpu.make_async_copy(g_ref, shard(0, sec), here.at[0]),
        pltpu.make_async_copy(ids_ref, ids_all.at[dp, z], here.at[1]),
        pltpu.make_async_copy(s_ref.at[z], s_all.at[dp, z], here.at[2]),
    ]
    for c in own:
        c.start()
    ids = [send(ids_ref, ids_all.at[dp, z], i_snd.at[0, 0], i_rcv.at[0, 0], to_mate)]
    for j in order:
        ids.append(send(ids_ref, ids_all.at[dp, z], i_snd.at[0, j], i_rcv.at[0, j], to_z[j]))
        ids.append(send(ids_ref, ids_all.at[dp, z], i_snd.at[1, j], i_rcv.at[1, j], other[j]))

    for j in order:
        a[j].wait_recv()
        x[j] = send(shard(j, sec), shard(j, sec), x_snd.at[j], x_rcv.at[j], to_x)
        y[j] = send(shard(j, sec), shard(j, sec), y_snd.at[j], y_rcv.at[j], to_y)
    s = {
        j: send(s_ref.at[(z + j) % 4], s_all.at[dp, z], s_snd.at[j], s_rcv.at[j], to_z[j])
        for j in order
    }
    d = {}
    for j in (0,) + order:
        if j % 2 == 0:
            x[j].wait_recv()
            d[j] = send(shard(j, sx), shard(j, sx), d_snd.at[j], d_rcv.at[j], to_y)
        else:
            y[j].wait_recv()
            d[j] = send(shard(j, sy), shard(j, sy), d_snd.at[j], d_rcv.at[j], to_x)
    for c in own:
        c.wait()
    h, f = [], []
    f.append(send(s_all.at[dp, z], s_all.at[dp, z], f_snd.at[0], f_rcv.at[0], to_mate))
    mate_cols = pl.ds(pl.multiple_of(mate * half, 128), half)
    for j in (0,) + order:
        (y if j % 2 == 0 else x)[j].wait_recv()
        d[j].wait_recv()
        h.append(
            send(g_all.at[zs[j], :, mate_cols], g_half.at[zs[j]], h_snd.at[j], h_rcv.at[j], to_mate)
        )
    for j in order:
        s[j].wait_recv()
        f.append(
            send(s_all.at[dp, zs[j]], s_all.at[dp, zs[j]], f_snd.at[j], f_rcv.at[j], to_mate)
        )
    for c in ids + h + f:
        c.wait_recv()
    for c in [*a.values(), *x.values(), *y.values(), *d.values(), *s.values(), *ids, *h, *f]:
        c.wait_send()


def spread_call(grad_out, ids_t, send_scaled):
    tok_count, width = grad_out.shape
    shapes = (
        jax.ShapeDtypeStruct((4, tok_count, 4 * width), BF),
        jax.ShapeDtypeStruct((4, tok_count, 2 * width), BF),
        jax.ShapeDtypeStruct((2, 4) + ids_t.shape, jnp.int32),
        jax.ShapeDtypeStruct((2,) + send_scaled.shape, BF),
    )
    vmem = pl.BlockSpec(memory_space=pltpu.VMEM)
    sems = [pltpu.SemaphoreType.DMA((4,))] * 14
    return pl.pallas_call(
        spread,
        out_shape=shapes,
        in_specs=[vmem] * 3,
        out_specs=(vmem,) * 4,
        scratch_shapes=[pltpu.SemaphoreType.DMA((3,))] + sems + [pltpu.SemaphoreType.DMA((2, 4))] * 2,
        compiler_params=pltpu.CompilerParams(
            collective_id=0, has_side_effects=True, vmem_limit_bytes=24 * 2**20
        ),
    )(grad_out, ids_t, send_scaled)


def local(grad_out, expert_ids, gate_weights, act, w_down):
    tok_count, top_count = expert_ids.shape
    hidden = act.shape[2]
    exp_dev = w_down.shape[0]
    experts = exp_dev * 4
    capacity = 3 * tok_count * top_count // (2 * experts)
    pairs = tok_count * top_count
    dp, z = lax.axis_index("dp"), lax.axis_index("expert")

    position = slots_of(expert_ids, experts, capacity).reshape(pairs)
    scaled = (gate_weights[:, :, None] * act.astype(F32)).astype(BF).reshape(pairs, hidden)
    slots = jnp.arange(experts * capacity, dtype=jnp.int32)
    place = (slots[:, None] == position[None, :]).astype(BF)
    send_scaled = jnp.dot(place, scaled, preferred_element_type=F32).astype(BF)
    send_scaled = send_scaled.reshape(4, exp_dev * capacity, hidden)

    g_all, g_half, ids_all, s_all = spread_call(grad_out, expert_ids.T, send_scaled)

    mine = z * exp_dev + jnp.arange(exp_dev, dtype=jnp.int32)
    named = jnp.any(ids_all[:, :, None] == mine[None, None, :, None, None], axis=3)
    earlier = jnp.arange(tok_count)[:, None] < jnp.arange(tok_count)[None, :]
    before = jnp.einsum(
        "rseu,ut->rset", named.astype(BF), earlier.astype(BF), preferred_element_type=F32
    ).astype(jnp.int32)
    before = jnp.where(named, before, -1)
    pick = (before[:, :, :, None, :] == jnp.arange(capacity)[:, None]).astype(BF)

    def rows_of(chosen, table):
        rows = jnp.einsum("sect,std->escd", chosen, table, preferred_element_type=F32)
        return rows.astype(BF).reshape(exp_dev, 4 * capacity, table.shape[2])

    pick_own = lax.dynamic_index_in_dim(pick, dp, 0, keepdims=False)
    pick_mate = lax.dynamic_index_in_dim(pick, 1 - dp, 0, keepdims=False)
    rows = rows_of(pick_own, g_all)
    half = g_half.shape[2]
    rows_half = lax.dynamic_slice_in_dim(rows, dp * half, half, 2)
    rows_mate = rows_of(pick_mate, g_half)

    unscaled = jnp.einsum("erd,ehd->erh", rows, w_down, preferred_element_type=F32).astype(BF)
    returning = jnp.transpose(unscaled.reshape(exp_dev, 4, capacity, hidden), (1, 0, 2, 3))
    back = []
    for j in range(4):
        block = lax.dynamic_index_in_dim(returning, (z + j) % 4, 0, keepdims=False)
        block = block.reshape(exp_dev * capacity, hidden)
        if j:
            block = lax.ppermute(block, "expert", [(i, (i + j) % 4) for i in range(4)])
        back.append(block)

    def by_expert(index):
        part = lax.dynamic_index_in_dim(s_all, index, 0, keepdims=False)
        part = part.reshape(4, exp_dev, capacity, hidden)
        return jnp.transpose(part, (1, 0, 2, 3)).reshape(exp_dev, 4 * capacity, hidden)

    scaled_rows = jnp.concatenate([by_expert(dp), by_expert(1 - dp)], axis=1)
    both = jnp.concatenate([rows_half, rows_mate], axis=1)
    grad_w = jnp.einsum("erh,erd->ehd", scaled_rows, both, preferred_element_type=F32).astype(BF)

    per_dev = exp_dev * capacity
    at = (z + 4 - position // per_dev) % 4 * per_dev + position % per_dev
    fetch = (at[:, None] == slots[None, :]).astype(BF)
    unscaled_tok = jnp.dot(fetch, jnp.concatenate(back, axis=0), preferred_element_type=F32)
    unscaled_tok = unscaled_tok.reshape(tok_count, top_count, hidden)
    grad_hidden = (gate_weights[:, :, None] * unscaled_tok).astype(BF)
    gate_share = jnp.sum(act.astype(F32) * unscaled_tok, axis=2)
    return (grad_hidden, lax.psum(gate_share, "section"), grad_w)


def solution(mesh):
    placed = (
        P(("dp", "expert"), "section"),
        P(("dp", "expert"), None),
        P(("dp", "expert"), None),
        P(("dp", "expert"), None, "section"),
        P("expert", "section", None),
    )
    sizes = tuple(mesh.shape[a] for a in ("dp", "section", "expert"))
    return jax.shard_map(
        local if sizes == (2, 4, 4) else local_general,
        mesh=mesh,
        in_specs=placed,
        out_specs=(
            P(("dp", "expert"), None, "section"),
            P(("dp", "expert"), None),
            P("expert", "section", "dp"),
        ),
        check_vma=False,
    )
```

time: 440 us -> 137 us (0.31)
  blocking collectives: 296 us -> 16 us
  Pallas kernels: 0 us -> 47.2 us
  waiting for transfers between devices: 40.6 us -> 0.01 us
  other arithmetic: 20.2 us -> 2.64 us
  between operations: 14.2 us -> 0.89 us
  matrix products: 34.9 us -> 43.4 us
  local copies, waits for them, and re-layouts: 30.2 us -> 23.8 us
    all_to_all x2 -> x0, blocking collectives: 265 us -> none  [the longest x1 243 us: local(): lax.all_to_all(send_grad, 'expert', split_axis=0, concat_axis=0, tiled=True)]
    pallas_call x0 -> x1, Pallas kernels: none -> 47.2 us  [spread_call(): pl.pallas_call(spread, out_shape=shapes, in_specs=[vmem] * 3, out_specs=(...]
    reduce_scatter x1 -> x0, waiting for transfers between devices: 21.8 us -> none  [local(): lax.psum_scatter(weight_part.astype(jnp.bfloat16), 'dp', scatter_dimensio...]
    all_to_all x1 -> x0, waiting for transfers between devices: 18.8 us -> none  [local(): lax.all_to_all(returning, 'expert', split_axis=0, concat_axis=0, tiled=True)]
    another operation x3 -> x0, other arithmetic: 18.2 us -> none
    gather x3 -> x0, local copies, waits for them, and re-layouts: 17.7 us -> none  [the longest x1 8.99 us: local(): rows_ext[token_index].reshape(experts, capacity, full_rows.shape[1])]
    all_gather x1 -> x0, blocking collectives: 15.9 us -> none  [local(): full_rows = lax.all_gather(grad_out, 'section', axis=1, tiled=True)]
    convert_element_type x0 -> x2, local copies, waits for them, and re-layouts: none -> 12.7 us  [rows_of(): return rows.astype(BF).reshape(exp_dev, 4 * capacity, table.shape[2])]
  transfers between devices with their start and end apart: 2 -> 3, of which waited for: 2 -> 0; matrix products, arithmetic and copies ran while one was open for 0% -> 16% of each run, Pallas kernels for 0% -> 0%
where the time goes in v1:
time: 137 us
  Pallas kernels  47.2 us (34%)
  matrix products  43.4 us (32%)
  local copies, waits for them, and re-layouts  23.8 us (17%)
  blocking collectives  16 us (12%)
  starting transfers between devices  2.85 us (2%)
  other arithmetic  2.64 us (2%)
    pallas_call x1, Pallas kernels, spread_call(): pl.pallas_call(spread, out_shape=shapes, in_specs=[vmem] * 3, out_specs=(...  47.2 us
    dot_general x1, matrix products, local(): jnp.einsum('erd,ehd->erh', rows, w_down, preferred_element_type=F32)  16.4 us
    psum x1, blocking collectives, local(): return (grad_hidden, lax.psum(gate_share, 'section'), grad_w)  16 us
    convert_element_type x2, local copies, waits for them, and re-layouts, rows_of(): return rows.astype(BF).reshape(exp_dev, 4 * capacity, table.shape[2])  12.7 us
    dot_general x2, matrix products, rows_of(): jnp.einsum('sect,std->escd', chosen, table, preferred_element_type=F32)  10.9 us
    dot_general x1, matrix products, local(): jnp.einsum('erh,erd->ehd', scaled_rows, both, preferred_element_type=F32)  10.3 us
    dynamic_slice x1, local copies, waits for them, and re-layouts, local(): rows_half = lax.dynamic_slice_in_dim(rows, dp * half, half, 2)  5.31 us
    unnamed x12, local copies, waits for them, and re-layouts  4.55 us
  transfers between devices with their start and end apart: 3, of which 0 were waited for; matrix products, arithmetic and copies ran while one was open for 16% of the time, Pallas kernels for 0%

profile of v1, /device:TPU:0, one launch (start us, length us, event | category | flops | bytes accessed | tf_op | source)
XLA Modules:
  0.0 136.6 jit_solution(15714776277051510993)
XLA Ops:
  0.7 0.8 copy.28
  1.5 0.7 fusion.31
  2.4 0.7 select_reduce_fusion
  3.2 0.7 convert_add_fusion
  4.1 2.4 %fusion.8 = bf16[1536,256]{1,0:T(8,128)(2,1)S(1)} fusion(s32[1024]{0:T(1024)S(1)} %reshape.111, bf16[128,8,256]{2,1,0:T(8,128)(2,1)} %param.8, f32[128,8]{1,0:T(8,128)S(1)} %copy.28), kind=kOutput, calls=%fused_computation.13 | convolution fusion | flops 808058880 | bytes 1318912 | tf_op jit(solution)/shard_map/dot_general | solution.py:203
  6.5 47.2 %shard_map.76 = (bf16[4,128,3584]{2,1,0:T(8,128)(2,1)S(1)}, bf16[4,128,1792]{2,1,0:T(8,128)(2,1)S(1)}, s32[2,4,8,128]{3,2,1,0:T(8,128)S(1)}, bf16[2,4,384,256]{3,2,1,0:T(8,128)(2,1)S(1)}) custom-call(bf16[128,896]{1,0:T(8,128)(2,1)S(1)} %copy-done, s32[8,128]{1,0:T(8,128)S(1)} %bitcast.52, bf16[4,384,256]{2,1,0:T(8,128)(2,1)S(1)} %bitcast.51), custom_call_target="tpu_custom_call" | custom-call | tf_op jit(solution)/shard_map/pallas_call | solution.py:178
  53.6 1.8 %copy-done.2 = bf16[4,128,3584]{2,1,0:T(8,128)(2,1)} copy-done((bf16[4,128,3584]{2,1,0:T(8,128)(2,1)}, bf16[4,128,3584]{2,1,0:T(8,128)(2,1)S(1)}, u32[]{:S(2)}) %copy-start.2) | copy-done | bytes 3670040
  55.4 1.2 copy-done.3
  56.7 0.2 compare_reduce_fusion
  56.9 0.1 fusion.14
  57.1 0.2 iota_compare_fusion.6
  57.3 7.9 %convert_bitcast_fusion = bf16[16,4,24,3584]{3,2,0,1:T(8,128)(2,1)} fusion(bf16[4,128,3584]{2,1,0:T(8,128)(2,1)} %copy-done.2, pred[2,4,16,24,128]{4,3,2,1,0:T(8,128)(4,1)S(1)} %iota_compare_fusion.6, s32[]{:T(128)S(6)} %select_n.85), kind=kOutput, calls=%fused_computation.4 | convolution fusion | flops 1414791168 | bytes 14876676 | tf_op jit(solution)/shard_map/sect,std->escd/dot_general | solution.py:218
  65.2 9.7 %copy.30 = bf16[16,4,24,3584]{3,2,1,0:T(8,128)(2,1)} copy(bf16[16,4,24,3584]{3,2,0,1:T(8,128)(2,1)} %convert_bitcast_fusion) | data formatting | bytes 22020096 | tf_op jit(solution)/shard_map/convert_element_type | solution.py:219
  74.9 16.4 %convolution_convert_fusion.1 = bf16[16,96,256]{2,1,0:T(8,128)(2,1)S(1)} fusion(bf16[16,96,3584]{2,1,0:T(8,128)(2,1)} %bitcast.53, bf16[16,256,3584]{2,1,0:T(8,128)(2,1)} %param.9), kind=kOutput, calls=%fused_computation.19 | convolution fusion | flops 2818965504 | bytes 41156608 | tf_op jit(solution)/shard_map/erd,ehd->erh/dot_general | solution.py:228
  91.3 0.8 constant_dynamic-slice_fusion.6
  92.0 2.3 %collective-permute-start.2 = (bf16[384,256]{1,0:T(8,128)(2,1)}, bf16[384,256]{1,0:T(8,128)(2,1)S(1)}, u32[]{:S(2)}, u32[]{:S(2)}) collective-permute-start(bf16[384,256]{1,0:T(8,128)(2,1)} %bitcast.14), channel_id=1, source_target_pairs={{0,3},{1,0},{2,1},{3,2},{4,7},{5,4},{6,5},{7,6},{8,11},{9,8},{10,9... | collective-permute-start | bytes 589832 | tf_op jit(solution)/shard_map/ppermute | solution.py:235
  94.3 0.6 collective-permute-start
  94.9 3.1 %convert_bitcast_fusion.1 = bf16[16,4,24,1792]{3,2,0,1:T(8,128)(2,1)S(1)} fusion(bf16[4,128,1792]{2,1,0:T(8,128)(2,1)} %copy-done.3, pred[2,4,16,24,128]{4,3,2,1,0:T(8,128)(4,1)S(1)} %iota_compare_fusion.6, s32[]{:T(128)S(6)} %select_n.94), kind=kOutput, calls=%fused_computation.9 | convolution fusion | flops 707395584 | bytes 7536644 | tf_op jit(solution)/shard_map/sect,std->escd/dot_general | solution.py:218
  98.0 3.0 %copy.33 = bf16[16,4,24,1792]{3,2,1,0:T(8,128)(2,1)} copy(bf16[16,4,24,1792]{3,2,0,1:T(8,128)(2,1)S(1)} %convert_bitcast_fusion.1) | data formatting | bytes 11010048 | tf_op jit(solution)/shard_map/convert_element_type | solution.py:219
  100.9 5.3 %constant_dynamic-slice_fusion = bf16[16,96,1792]{2,1,0:T(8,128)(2,1)} fusion(bf16[16,96,3584]{2,1,0:T(8,128)(2,1)} %bitcast.54, s32[]{:T(128)S(6)} %select_n.95), kind=kLoop, calls=%fused_computation.62 | loop fusion | bytes 11010052 | tf_op jit(solution)/shard_map/dynamic_slice | solution.py:225
  106.6 10.3 %convolution_convert_fusion = bf16[16,256,1792]{2,1,0:T(8,128)(2,1)} fusion(bf16[16,96,1792]{2,1,0:T(8,128)(2,1)} %bitcast.55, bf16[16,96,1792]{2,1,0:T(8,128)(2,1)} %constant_dynamic-slice_fusion, bf16[16,96,256]{2,1,0:T(8,128)(2,1)S(1)} %bitcast.59, bf16[16,96,256]{2,1,0:T(8,128)(2,1)S(1)} %bitcast.60), kind=kOutput, calls=%fused_computation | convolution fusion | flops 2851078144 | bytes 27262976 | tf_op jit(solution)/shard_map/erh,erd->ehd/dot_general | solution.py:245
  116.9 3.1 %fusion.16 = (f32[128,8]{1,0:T(8,128)S(1)}, bf16[128,8,256]{2,1,0:T(8,128)(2,1)}) fusion(bf16[128,8,256]{2,1,0:T(8,128)(2,1)S(1)} %copy-done.4, f32[128,8]{1,0:T(8,128)S(1)} %copy.28, bf16[384,256]{1,0:T(8,128)(2,1)S(1)} %collective-permute-done.2, bf16[384,256]{1,0:T(8,128)(2,1)} %collective-permute-done.1, bf16[384,256]{1,0:T(8,128)(2,1)} %collective-permute-done, ...), kind=kOutput, calls=%fused_computation.26 | convolution fusion | flops 811334656 | bytes 1847296 | tf_op jit(solution)/shard_map/dot_general | solution.py:250
  120.0 16.0 %psum.7 = f32[128,8]{1,0:T(8,128)S(1)} all-reduce(f32[128,8]{1,0:T(8,128)S(1)} %get-tuple-element.19), channel_id=1, replica_groups=mesh['dp'=2,'section'=4,'expert'=4] {'section'}, use_global_device_ids=true, to_apply=%region_4.5 | all-reduce | flops 1024 | bytes 8192 | tf_op jit(solution)/shard_map/psum | solution.py:254
  136.0 0.7 copy.34
  (20 shorter events, 0.7 us)
Async XLA Ops:
  0.6 5.8 %copy-start.1 = (s32[128,8]{0,1:T(8,128)S(1)}, s32[128,8]{0,1:T(8,128)}, u32[]{:S(2)}) copy-start(s32[128,8]{0,1:T(8,128)} %param.6) | copy-start | bytes 12292
  0.6 5.8 %copy-start = (bf16[128,896]{1,0:T(8,128)(2,1)S(1)}, bf16[128,896]{1,0:T(8,128)(2,1)}, u32[]{:S(2)}) copy-start(bf16[128,896]{1,0:T(8,128)(2,1)} %g_ref.1) | copy-start | bytes 688132
  53.6 1.8 %copy-start.2 = (bf16[4,128,3584]{2,1,0:T(8,128)(2,1)}, bf16[4,128,3584]{2,1,0:T(8,128)(2,1)S(1)}, u32[]{:S(2)}) copy-start(bf16[4,128,3584]{2,1,0:T(8,128)(2,1)S(1)} %get-tuple-element.7) | copy-start | bytes 11010052
  55.4 1.2 copy-start.3
  92.0 24.8 %collective-permute-start.2 = (bf16[384,256]{1,0:T(8,128)(2,1)}, bf16[384,256]{1,0:T(8,128)(2,1)S(1)}, u32[]{:S(2)}, u32[]{:S(2)}) collective-permute-start(bf16[384,256]{1,0:T(8,128)(2,1)} %bitcast.14), channel_id=1, source_target_pairs={{0,3},{1,0},{2,1},{3,2},{4,7},{5,4},{6,5},{7,6},{8,11},{9,8},{10,9... | collective-permute-start | bytes 589832 | tf_op jit(solution)/shard_map/ppermute | solution.py:235
  94.3 22.5 %collective-permute-start.1 = (bf16[384,256]{1,0:T(8,128)(2,1)S(1)}, bf16[384,256]{1,0:T(8,128)(2,1)}, u32[]{:S(2)}, u32[]{:S(2)}) collective-permute-start(bf16[384,256]{1,0:T(8,128)(2,1)S(1)} %bitcast.63), channel_id=1, source_target_pairs={{0,2},{1,3},{2,0},{3,1},{4,6},{5,7},{6,4},{7,5},{8,10},{9,11},{10,... | collective-permute-start | bytes 589832 | tf_op jit(solution)/shard_map/ppermute | solution.py:235
  94.3 22.5 %collective-permute-start = (bf16[384,256]{1,0:T(8,128)(2,1)S(1)}, bf16[384,256]{1,0:T(8,128)(2,1)}, u32[]{:S(2)}, u32[]{:S(2)}) collective-permute-start(bf16[384,256]{1,0:T(8,128)(2,1)S(1)} %bitcast.62), channel_id=1, source_target_pairs={{0,1},{1,2},{2,3},{3,0},{4,5},{5,6},{6,7},{7,4},{8,9},{9,10},{10,1... | collective-permute-start | bytes 589832 | tf_op jit(solution)/shard_map/ppermute | solution.py:235
  106.5 10.3 %copy-start.4 = (bf16[128,8,256]{2,1,0:T(8,128)(2,1)S(1)}, bf16[128,8,256]{2,1,0:T(8,128)(2,1)}, u32[]{:S(2)}) copy-start(bf16[128,8,256]{2,1,0:T(8,128)(2,1)} %param.8) | copy-start | bytes 1572868

commit v2 on v1

--- a/solution.py
+++ b/solution.py
@@ -76,9 +76,8 @@
 
 
 def spread(
-    g_ref, ids_ref, s_ref, g_all, g_half, ids_all, s_all, here,
-    a_snd, a_rcv, x_snd, x_rcv, y_snd, y_rcv, d_snd, d_rcv, h_snd, h_rcv,
-    s_snd, s_rcv, f_snd, f_rcv, i_snd, i_rcv,
+    g_ref, ids_ref, g_all, g_half, ids_all, here,
+    a_snd, a_rcv, x_snd, x_rcv, y_snd, y_rcv, d_snd, d_rcv, h_snd, h_rcv, i_snd, i_rcv,
 ):
     dp, sec, z = (lax.axis_index(a) for a in ("dp", "section", "expert"))
     width = g_ref.shape[1]
@@ -103,38 +102,28 @@
         copy.start()
         return copy
 
-    def cols(s):
-        return pl.ds(pl.multiple_of(s * width, 128), width)
-
-    zs = [(z + 4 - j) % 4 for j in range(4)]
-
     def shard(j, s):
-        return g_all.at[zs[j], :, cols(s)]
+        return g_all.at[j, :, pl.ds(pl.multiple_of(s * width, 128), width)]
 
     order = (1, 3, 2)
-    a = {j: send(g_ref, shard(0, sec), a_snd.at[j], a_rcv.at[j], to_z[j]) for j in order}
+    a = {j: send(g_ref, shard(j, sec), a_snd.at[j], a_rcv.at[j], to_z[j]) for j in order}
     x = {0: send(g_ref, shard(0, sec), x_snd.at[0], x_rcv.at[0], to_x)}
     y = {0: send(g_ref, shard(0, sec), y_snd.at[0], y_rcv.at[0], to_y)}
     own = [
         pltpu.make_async_copy(g_ref, shard(0, sec), here.at[0]),
-        pltpu.make_async_copy(ids_ref, ids_all.at[dp, z], here.at[1]),
-        pltpu.make_async_copy(s_ref.at[z], s_all.at[dp, z], here.at[2]),
+        pltpu.make_async_copy(ids_ref, ids_all.at[0, 0], here.at[1]),
     ]
     for c in own:
         c.start()
-    ids = [send(ids_ref, ids_all.at[dp, z], i_snd.at[0, 0], i_rcv.at[0, 0], to_mate)]
+    ids = [send(ids_ref, ids_all.at[1, 0], i_snd.at[1, 0], i_rcv.at[1, 0], to_mate)]
     for j in order:
-        ids.append(send(ids_ref, ids_all.at[dp, z], i_snd.at[0, j], i_rcv.at[0, j], to_z[j]))
-        ids.append(send(ids_ref, ids_all.at[dp, z], i_snd.at[1, j], i_rcv.at[1, j], other[j]))
+        ids.append(send(ids_ref, ids_all.at[0, j], i_snd.at[0, j], i_rcv.at[0, j], to_z[j]))
+        ids.append(send(ids_ref, ids_all.at[1, j], i_snd.at[1, j], i_rcv.at[1, j], other[j]))
 
     for j in order:
         a[j].wait_recv()
         x[j] = send(shard(j, sec), shard(j, sec), x_snd.at[j], x_rcv.at[j], to_x)
         y[j] = send(shard(j, sec), shard(j, sec), y_snd.at[j], y_rcv.at[j], to_y)
-    s = {
-        j: send(s_ref.at[(z + j) % 4], s_all.at[dp, z], s_snd.at[j], s_rcv.at[j], to_z[j])
-        for j in order
-    }
     d = {}
     for j in (0,) + order:
         if j % 2 == 0:
@@ -145,46 +134,141 @@
             d[j] = send(shard(j, sy), shard(j, sy), d_snd.at[j], d_rcv.at[j], to_x)
     for c in own:
         c.wait()
-    h, f = [], []
-    f.append(send(s_all.at[dp, z], s_all.at[dp, z], f_snd.at[0], f_rcv.at[0], to_mate))
+    h = []
     mate_cols = pl.ds(pl.multiple_of(mate * half, 128), half)
     for j in (0,) + order:
         (y if j % 2 == 0 else x)[j].wait_recv()
         d[j].wait_recv()
-        h.append(
-            send(g_all.at[zs[j], :, mate_cols], g_half.at[zs[j]], h_snd.at[j], h_rcv.at[j], to_mate)
-        )
-    for j in order:
-        s[j].wait_recv()
-        f.append(
-            send(s_all.at[dp, zs[j]], s_all.at[dp, zs[j]], f_snd.at[j], f_rcv.at[j], to_mate)
-        )
-    for c in ids + h + f:
+        h.append(send(g_all.at[j, :, mate_cols], g_half.at[j], h_snd.at[j], h_rcv.at[j], to_mate))
+    for c in ids + h:
         c.wait_recv()
-    for c in [*a.values(), *x.values(), *y.values(), *d.values(), *s.values(), *ids, *h, *f]:
+    for c in [*a.values(), *x.values(), *y.values(), *d.values(), *ids, *h]:
         c.wait_send()
 
 
-def spread_call(grad_out, ids_t, send_scaled):
+VMEM = pl.BlockSpec(memory_space=pltpu.VMEM)
+
+
+def spread_call(grad_out, ids_t):
     tok_count, width = grad_out.shape
     shapes = (
         jax.ShapeDtypeStruct((4, tok_count, 4 * width), BF),
         jax.ShapeDtypeStruct((4, tok_count, 2 * width), BF),
         jax.ShapeDtypeStruct((2, 4) + ids_t.shape, jnp.int32),
-        jax.ShapeDtypeStruct((2,) + send_scaled.shape, BF),
-    )
-    vmem = pl.BlockSpec(memory_space=pltpu.VMEM)
-    sems = [pltpu.SemaphoreType.DMA((4,))] * 14
+    )
     return pl.pallas_call(
         spread,
         out_shape=shapes,
-        in_specs=[vmem] * 3,
-        out_specs=(vmem,) * 4,
-        scratch_shapes=[pltpu.SemaphoreType.DMA((3,))] + sems + [pltpu.SemaphoreType.DMA((2, 4))] * 2,
+        in_specs=[VMEM] * 2,
+        out_specs=(VMEM,) * 3,
+        scratch_shapes=[pltpu.SemaphoreType.DMA((2,))]
+        + [pltpu.SemaphoreType.DMA((4,))] * 10
+        + [pltpu.SemaphoreType.DMA((2, 4))] * 2,
         compiler_params=pltpu.CompilerParams(
             collective_id=0, has_side_effects=True, vmem_limit_bytes=24 * 2**20
         ),
-    )(grad_out, ids_t, send_scaled)
+    )(grad_out, ids_t)
+
+
+def widen(wide, tight, per_wide, per_tight, flip):
+    shape = (tight, wide) if flip else (wide, tight)
+    row = lax.broadcasted_iota(jnp.int32, shape, 1 if flip else 0)
+    col = lax.broadcasted_iota(jnp.int32, shape, 0 if flip else 1)
+    slot = row % per_wide
+    same = (slot < per_tight) & (row // per_wide * per_tight + slot == col)
+    return jnp.where(same, 1.0, 0.0).astype(BF)
+
+
+def expand(pick, table, rows, cols, tile):
+    @pl.loop(0, cols // tile)
+    def _(i):
+        at = pl.ds(pl.multiple_of(i * tile, 128), tile)
+        rows[:, at] = jnp.dot(pick[...], table[:, at], preferred_element_type=F32).astype(BF)
+
+
+def hidden_kernel(padded, capacity, pick, g_all, w_ref, out, rows, wide):
+    e = pl.program_id(0)
+
+    @pl.when(e == 0)
+    def _():
+        for s in range(4):
+            expand(pick.at[s], g_all.at[s], rows.at[s], g_all.shape[2], 512)
+
+    at = pl.ds(pl.multiple_of(e * padded, padded), padded)
+    mine = jnp.concatenate([rows[s, at, :] for s in range(4)], axis=0)
+    unscaled = lax.dot_general(
+        mine, w_ref[0], (((1,), (1,)), ((), ())), preferred_element_type=F32
+    ).astype(BF)
+    for s in range(4):
+        wide[s, at, :] = unscaled[s * padded : (s + 1) * padded]
+
+    @pl.when(e == pl.num_programs(0) - 1)
+    def _():
+        tighten = widen(wide.shape[1], out.shape[1], padded, capacity, True)
+        for s in range(4):
+            out[s] = jnp.dot(tighten, wide[s], preferred_element_type=F32).astype(BF)
+
+
+def hidden_call(pick, g_all, w_down, capacity):
+    exp_dev, hidden, width = w_down.shape
+    padded = pick.shape[1] // exp_dev
+    return pl.pallas_call(
+        functools.partial(hidden_kernel, padded, capacity),
+        grid=(exp_dev,),
+        out_shape=jax.ShapeDtypeStruct((4, exp_dev * capacity, hidden), BF),
+        in_specs=[VMEM, VMEM, pl.BlockSpec((1, hidden, width), lambda e: (e, 0, 0))],
+        out_specs=VMEM,
+        scratch_shapes=[
+            pltpu.VMEM((4, exp_dev * padded, width), BF),
+            pltpu.VMEM((4, exp_dev * padded, hidden), BF),
+        ],
+        compiler_params=pltpu.CompilerParams(vmem_limit_bytes=28 * 2**20),
+        cost_estimate=pl.CostEstimate(
+            flops=8 * exp_dev * padded * hidden * width, bytes_accessed=w_down.size * 2, transcendentals=0
+        ),
+    )(pick, g_all, w_down)
+
+
+def weight_kernel(padded, capacity, dp_ref, pick, g_all, g_half, s_own, s_mate, out, rows, wide):
+    e = pl.program_id(0)
+    half = g_half.shape[2]
+
+    @pl.when(e == 0)
+    def _():
+        cols = pl.ds(pl.multiple_of(dp_ref[0] * half, 128), half)
+        loosen = widen(wide.shape[1], s_own.shape[1], padded, capacity, False)
+        for s in range(4):
+            expand(pick.at[0, s], g_all.at[s, :, cols], rows.at[s], half, 256)
+            expand(pick.at[1, s], g_half.at[s], rows.at[4 + s], half, 256)
+            wide[s] = jnp.dot(loosen, s_own[s], preferred_element_type=F32).astype(BF)
+            wide[4 + s] = jnp.dot(loosen, s_mate[s], preferred_element_type=F32).astype(BF)
+
+    at = pl.ds(pl.multiple_of(e * padded, padded), padded)
+    grads = jnp.concatenate([rows[s, at, :] for s in range(8)], axis=0)
+    scaled = jnp.concatenate([wide[s, at, :] for s in range(8)], axis=0)
+    out[0] = lax.dot_general(
+        scaled, grads, (((0,), (0,)), ((), ())), preferred_element_type=F32
+    ).astype(BF)
+
+
+def weight_call(dp, pick, g_all, g_half, s_own, s_mate, exp_dev, capacity):
+    padded = pick.shape[2] // exp_dev
+    half, hidden = g_half.shape[2], s_own.shape[2]
+    return pl.pallas_call(
+        functools.partial(weight_kernel, padded, capacity),
+        grid=(exp_dev,),
+        out_shape=jax.ShapeDtypeStruct((exp_dev, hidden, half), BF),
+        in_specs=[pl.BlockSpec(memory_space=pltpu.SMEM)] + [VMEM] * 5,
+        out_specs=pl.BlockSpec((1, hidden, half), lambda e: (e, 0, 0)),
+        scratch_shapes=[
+            pltpu.VMEM((8, exp_dev * padded, half), BF),
+            pltpu.VMEM((8, exp_dev * padded, hidden), BF),
+        ],
+        compiler_params=pltpu.CompilerParams(vmem_limit_bytes=28 * 2**20),
+        cost_estimate=pl.CostEstimate(
+            flops=16 * exp_dev * padded * hidden * half, bytes_accessed=exp_dev * hidden * half * 2, transcendentals=0
+        ),
+    )(dp, pick, g_all, g_half, s_own, s_mate)
 
 
 def local(grad_out, expert_ids, gate_weights, act, w_down):
@@ -193,17 +277,28 @@
     exp_dev = w_down.shape[0]
     experts = exp_dev * 4
     capacity = 3 * tok_count * top_count // (2 * experts)
+    padded = -(-capacity // 32) * 32
     pairs = tok_count * top_count
+    per_dev = exp_dev * capacity
     dp, z = lax.axis_index("dp"), lax.axis_index("expert")
 
-    position = slots_of(expert_ids, experts, capacity).reshape(pairs)
+    g_all, g_half, ids_all = spread_call(grad_out, expert_ids.T)
+
+    first = expert_ids - z * exp_dev
+    first = jnp.where(first < 0, first + experts, first)
+    position = slots_of(first, experts, capacity).reshape(pairs)
     scaled = (gate_weights[:, :, None] * act.astype(F32)).astype(BF).reshape(pairs, hidden)
     slots = jnp.arange(experts * capacity, dtype=jnp.int32)
     place = (slots[:, None] == position[None, :]).astype(BF)
     send_scaled = jnp.dot(place, scaled, preferred_element_type=F32).astype(BF)
-    send_scaled = send_scaled.reshape(4, exp_dev * capacity, hidden)
-
-    g_all, g_half, ids_all, s_all = spread_call(grad_out, expert_ids.T, send_scaled)
+    send_scaled = send_scaled.reshape(4, per_dev, hidden)
+    send_scaled, g_all, ids_all = lax.optimization_barrier((send_scaled, g_all, ids_all))
+    s_own = [
+        lax.ppermute(send_scaled[j], "expert", [(i, (i + j) % 4) for i in range(4)])
+        if j
+        else send_scaled[0]
+        for j in range(4)
+    ]
 
     mine = z * exp_dev + jnp.arange(exp_dev, dtype=jnp.int32)
     named = jnp.any(ids_all[:, :, None] == mine[None, None, :, None, None], axis=3)
@@ -212,46 +307,31 @@
         "rseu,ut->rset", named.astype(BF), earlier.astype(BF), preferred_element_type=F32
     ).astype(jnp.int32)
     before = jnp.where(named, before, -1)
-    pick = (before[:, :, :, None, :] == jnp.arange(capacity)[:, None]).astype(BF)
-
-    def rows_of(chosen, table):
-        rows = jnp.einsum("sect,std->escd", chosen, table, preferred_element_type=F32)
-        return rows.astype(BF).reshape(exp_dev, 4 * capacity, table.shape[2])
-
-    pick_own = lax.dynamic_index_in_dim(pick, dp, 0, keepdims=False)
-    pick_mate = lax.dynamic_index_in_dim(pick, 1 - dp, 0, keepdims=False)
-    rows = rows_of(pick_own, g_all)
-    half = g_half.shape[2]
-    rows_half = lax.dynamic_slice_in_dim(rows, dp * half, half, 2)
-    rows_mate = rows_of(pick_mate, g_half)
-
-    unscaled = jnp.einsum("erd,ehd->erh", rows, w_down, preferred_element_type=F32).astype(BF)
-    returning = jnp.transpose(unscaled.reshape(exp_dev, 4, capacity, hidden), (1, 0, 2, 3))
-    back = []
-    for j in range(4):
-        block = lax.dynamic_index_in_dim(returning, (z + j) % 4, 0, keepdims=False)
-        block = block.reshape(exp_dev * capacity, hidden)
-        if j:
-            block = lax.ppermute(block, "expert", [(i, (i + j) % 4) for i in range(4)])
-        back.append(block)
-
-    def by_expert(index):
-        part = lax.dynamic_index_in_dim(s_all, index, 0, keepdims=False)
-        part = part.reshape(4, exp_dev, capacity, hidden)
-        return jnp.transpose(part, (1, 0, 2, 3)).reshape(exp_dev, 4 * capacity, hidden)
-
-    scaled_rows = jnp.concatenate([by_expert(dp), by_expert(1 - dp)], axis=1)
-    both = jnp.concatenate([rows_half, rows_mate], axis=1)
-    grad_w = jnp.einsum("erh,erd->ehd", scaled_rows, both, preferred_element_type=F32).astype(BF)
-
-    per_dev = exp_dev * capacity
-    at = (z + 4 - position // per_dev) % 4 * per_dev + position % per_dev
-    fetch = (at[:, None] == slots[None, :]).astype(BF)
+    pick = (before[:, :, :, None, :] == jnp.arange(padded)[:, None]).astype(BF)
+    pick = pick.reshape(2, 4, exp_dev * padded, tok_count)
+
+    returning = hidden_call(pick[0], g_all, w_down, capacity)
+    s_own, returning = lax.optimization_barrier((s_own, returning))
+    s_own = jnp.stack(s_own)
+    s_mate = lax.ppermute(s_own, "dp", [(0, 1), (1, 0)])
+    back = [
+        lax.ppermute(returning[j], "expert", [(i, (i - j) % 4) for i in range(4)])
+        if j
+        else returning[0]
+        for j in range(4)
+    ]
+    grad_w = weight_call(
+        dp.astype(jnp.int32).reshape(1), pick, g_all, g_half, s_own, s_mate, exp_dev, capacity
+    )
+
+    back, grad_w = lax.optimization_barrier((back, grad_w))
+    fetch = (position[:, None] == slots[None, :]).astype(BF)
     unscaled_tok = jnp.dot(fetch, jnp.concatenate(back, axis=0), preferred_element_type=F32)
     unscaled_tok = unscaled_tok.reshape(tok_count, top_count, hidden)
     grad_hidden = (gate_weights[:, :, None] * unscaled_tok).astype(BF)
-    gate_share = jnp.sum(act.astype(F32) * unscaled_tok, axis=2)
-    return (grad_hidden, lax.psum(gate_share, "section"), grad_w)
+    share = jnp.sum(act.astype(F32) * unscaled_tok, axis=2)
+    other = [lax.ppermute(share, "section", [(i, i ^ m) for i in range(4)]) for m in (1, 2, 3)]
+    return (grad_hidden, (share + other[0]) + (other[1] + other[2]), grad_w)
 
 
 def solution(mesh):

time: 137 us -> 130 us (0.949)
  Pallas kernels: 47.2 us -> 100 us
  matrix products: 43.4 us -> 5.15 us
  local copies, waits for them, and re-layouts: 23.8 us -> 5.51 us
  blocking collectives: 16 us -> 0 us
  starting transfers between devices: 2.85 us -> 11.9 us
  waiting for transfers between devices: 0.01 us -> 3.09 us
    pallas_call x1 -> x3, Pallas kernels: 47.2 us -> 100 us  [the longest x1 46 us: spread_call(): pl.pallas_call(spread, out_shape=shapes, in_specs=[VMEM] * 2, out_specs=(...]
    dot_general x4 -> x0, matrix products: 37.6 us -> none  [the longest x1 16.4 us: local(): jnp.einsum('erd,ehd->erh', rows, w_down, preferred_element_type=F32)]
    psum x1 -> x0, blocking collectives: 16 us -> none  [local(): return (grad_hidden, lax.psum(gate_share, 'section'), grad_w)]
    convert_element_type x2 -> x0, local copies, waits for them, and re-layouts: 12.7 us -> none  [rows_of(): return rows.astype(BF).reshape(exp_dev, 4 * capacity, table.shape[2])]
    ppermute x3 -> x10, starting transfers between devices: 2.85 us -> 11.9 us  [the longest x3 5.36 us: local(): lax.ppermute(returning[j], 'expert', [(i, (i - j) % 4) for i in range(4)])]
    dynamic_slice x2 -> x0, local copies, waits for them, and re-layouts: 5.41 us -> none  [the longest x1 5.31 us: local(): rows_half = lax.dynamic_slice_in_dim(rows, dp * half, half, 2)]
    ppermute x3 -> x10, waiting for transfers between devices: 0.01 us -> 3.09 us  [the longest x3 3.07 us: local(): lax.ppermute(share, 'section', [(i, i ^ m) for i in range(4)])]
  transfers between devices with their start and end apart: 3 -> 10, of which waited for: 0 -> 3; matrix products, arithmetic and copies ran while one was open for 16% -> 1% of each run, Pallas kernels for 0% -> 42%
where the time goes in v2:
time: 130 us; the launch traced here: 129 us
  Pallas kernels  100 us (77%)
  starting transfers between devices  11.9 us (9%)
  local copies, waits for them, and re-layouts  5.51 us (4%)
  matrix products  5.15 us (4%)
  waiting for transfers between devices  3.09 us (2%)
  other arithmetic  2.27 us (2%)
    pallas_call x1, Pallas kernels, spread_call(): pl.pallas_call(spread, out_shape=shapes, in_specs=[VMEM] * 2, out_specs=(...  46 us
    pallas_call x1, Pallas kernels, hidden_call(): pl.pallas_call(functools.partial(hidden_kernel, padded, capacity), grid=(...  27.8 us
    pallas_call x1, Pallas kernels, weight_call(): pl.pallas_call(functools.partial(weight_kernel, padded, capacity), grid=(...  26.5 us
    ppermute x3, starting transfers between devices, local(): lax.ppermute(returning[j], 'expert', [(i, (i - j) % 4) for i in range(4)])  5.36 us
    unnamed x12, local copies, waits for them, and re-layouts  5.12 us
    ppermute x3, starting transfers between devices, local(): lax.ppermute(share, 'section', [(i, i ^ m) for i in range(4)])  3.49 us
    ppermute x3, waiting for transfers between devices, local(): lax.ppermute(share, 'section', [(i, i ^ m) for i in range(4)])  3.07 us
    ppermute x3, starting transfers between devices, local(): lax.ppermute(send_scaled[j], 'expert', [(i, (i + j) % 4) for i in range(4)])  2.97 us
  transfers between devices with their start and end apart: 10, of which 3 were waited for; matrix products, arithmetic and copies ran while one was open for 1% of the time, Pallas kernels for 42%

profile of v2, /device:TPU:0, one launch (start us, length us, event | category | flops | bytes accessed | tf_op | source)
XLA Modules:
  0.0 129.1 jit_solution(13075414782191643767)
XLA Ops:
  0.6 0.7 compare_select_fusion
  1.6 0.7 convert_add_fusion
  2.5 0.8 copy.20
  3.3 0.9 copy-done.2
  4.2 0.7 copy-done.3
  4.9 46.0 %shard_map.76 = (bf16[4,128,3584]{2,1,0:T(8,128)(2,1)S(1)}, bf16[4,128,1792]{2,1,0:T(8,128)(2,1)S(1)}, s32[2,4,8,128]{3,2,1,0:T(8,128)S(1)}) custom-call(bf16[128,896]{1,0:T(8,128)(2,1)S(1)} %copy-done.2, s32[8,128]{1,0:T(8,128)S(1)} %bitcast.41), custom_call_target="tpu_custom_call" | custom-call | tf_op jit(solution)/shard_map/pallas_call | solution.py:159
  50.9 2.8 %fusion.4 = bf16[1536,256]{1,0:T(8,128)(2,1)S(1)} fusion(s32[1024]{0:T(1024)S(1)} %eq.81, bf16[128,8,256]{2,1,0:T(8,128)(2,1)} %param.8, f32[128,8]{1,0:T(8,128)S(1)} %copy.20), kind=kOutput, calls=%fused_computation.6 | convolution fusion | flops 808058880 | bytes 1318912 | tf_op jit(solution)/shard_map/dot_general | solution.py:293
  53.8 2.3 %collective-permute-start.2 = (bf16[384,256]{1,0:T(8,128)(2,1)S(1)}, bf16[384,256]{1,0:T(8,128)(2,1)S(1)}, u32[]{:S(2)}, u32[]{:S(2)}) collective-permute-start(bf16[384,256]{1,0:T(8,128)(2,1)S(1)} %get-tuple-element.47), channel_id=1, source_target_pairs={{0,3},{1,0},{2,1},{3,2},{4,7},{5,4},{6,5},{7,6},{8,11},{9,8},{10,9... | collective-permute-start | bytes 589832 | tf_op jit(solution)/shard_map/ppermute | solution.py:297
  56.1 0.6 collective-permute-start
  57.3 27.8 %shard_map.77 = bf16[4,384,256]{2,1,0:T(8,128)(2,1)S(1)} custom-call(bf16[4,512,128]{2,1,0:T(8,128)(2,1)S(1)} %bitcast.40, bf16[4,128,3584]{2,1,0:T(8,128)(2,1)S(1)} %get-tuple-element.23.g_all, bf16[16,256,3584]{2,1,0:T(8,128)(2,1)} %w_ref.1), custom_call_target="tpu_custom_call" | custom-call | flops 3758096384 | bytes 29360128 | tf_op jit(solution)/shard_map/pallas_call | solution.py:215
  85.4 0.3 fusion.5.pick
  85.8 2.9 %collective-permute-start.5 = (bf16[384,256]{1,0:T(8,128)(2,1)S(1)}, bf16[384,256]{1,0:T(8,128)(2,1)S(1)}, u32[]{:S(2)}, u32[]{:S(2)}) collective-permute-start(bf16[384,256]{1,0:T(8,128)(2,1)S(1)} %get-tuple-element.43), channel_id=1, source_target_pairs={{0,1},{1,2},{2,3},{3,0},{4,5},{5,6},{6,7},{7,4},{8,9},{9,10},{10,1... | collective-permute-start | bytes 589832 | tf_op jit(solution)/shard_map/ppermute | solution.py:318
  88.7 0.9 collective-permute-start.4
  89.6 1.5 %collective-permute-start.3 = (bf16[384,256]{1,0:T(8,128)(2,1)S(1)}, bf16[384,256]{1,0:T(8,128)(2,1)S(1)}, u32[]{:S(2)}, u32[]{:S(2)}) collective-permute-start(bf16[384,256]{1,0:T(8,128)(2,1)S(1)} %get-tuple-element.45), channel_id=1, source_target_pairs={{0,3},{1,0},{2,1},{3,2},{4,7},{5,4},{6,5},{7,6},{8,11},{9,8},{10,9... | collective-permute-start | bytes 589832 | tf_op jit(solution)/shard_map/ppermute | solution.py:318
  91.2 2.0 %copy-done.1 = bf16[4,128,3584]{2,1,0:T(8,128)(2,1)S(1)} copy-done((bf16[4,128,3584]{2,1,0:T(8,128)(2,1)S(1)}, bf16[4,128,3584]{2,1,0:T(8,128)(2,1)}, u32[]{:S(2)}) %copy-start.1) | copy-done | bytes 3670040
  93.2 26.5 %shard_map.78 = bf16[16,256,1792]{2,1,0:T(8,128)(2,1)} custom-call(s32[1]{0:T(128)} %bitcast.14.dp_ref, bf16[2,4,512,128]{3,2,1,0:T(8,128)(2,1)S(1)} %fusion.5.pick, bf16[4,128,3584]{2,1,0:T(8,128)(2,1)S(1)} %copy-done.1, bf16[4,128,1792]{2,1,0:T(8,128)(2,1)S(1)} %get-tuple-element.25.g_half, bf16[4,384,256]{2,1,0:T(8,128)(2,1)S(1)} %pad_maximum_fusion.s_own, ...), custom_call_target="tpu_custom_call" | custom-call | flops 3758096384 | bytes 14680064 | tf_op jit(solution)/shard_map/pallas_call | solution.py:257
  119.8 2.1 %fusion.9 = (f32[128,8]{1,0:T(8,128)S(1)}, bf16[128,8,256]{2,1,0:T(8,128)(2,1)}) fusion(bf16[128,8,256]{2,1,0:T(8,128)(2,1)S(1)} %copy-done.4, f32[128,8]{1,0:T(8,128)S(1)} %copy.20, bf16[384,256]{1,0:T(8,128)(2,1)S(1)} %collective-permute-done.5, bf16[384,256]{1,0:T(8,128)(2,1)S(1)} %collective-permute-done.4, ...), kind=kOutput, calls=%fused_computation.15 | convolution fusion | flops 811334656 | bytes 1847296 | tf_op jit(solution)/shard_map/dot_general | solution.py:329
  121.9 1.5 %collective-permute-start.9 = (f32[128,8]{1,0:T(8,128)S(1)}, f32[128,8]{1,0:T(8,128)S(1)}, u32[]{:S(2)}, u32[]{:S(2)}) collective-permute-start(f32[128,8]{1,0:T(8,128)S(1)} %get-tuple-element.41), channel_id=1, source_target_pairs={{0,12},{4,8},{8,4},{12,0},{1,13},{5,9},{9,5},{13,1},{2,14},{6,10},... | collective-permute-start | bytes 12296 | tf_op jit(solution)/shard_map/ppermute | solution.py:333
  123.3 0.8 collective-permute-start.8
  124.1 1.2 collective-permute-start.7
  125.3 2.1 %collective-permute-done.9 = f32[128,8]{1,0:T(8,128)S(1)} collective-permute-done((f32[128,8]{1,0:T(8,128)S(1)}, f32[128,8]{1,0:T(8,128)S(1)}, u32[]{:S(2)}, u32[]{:S(2)}) %collective-permute-start.9) | collective-permute-done | bytes 4128 | tf_op jit(solution)/shard_map/ppermute | solution.py:333
  127.4 0.6 collective-permute-done.8
  128.0 0.4 collective-permute-done.7
  128.4 0.7 copy.22
  (32 shorter events, 1.4 us)
Async XLA Ops:
  3.3 0.9 copy-start.2
  4.2 0.7 copy-start.3
  50.9 6.4 %copy-start = (bf16[4,128,3584]{2,1,0:T(8,128)(2,1)}, bf16[4,128,3584]{2,1,0:T(8,128)(2,1)S(1)}, u32[]{:S(2)}) copy-start(bf16[4,128,3584]{2,1,0:T(8,128)(2,1)S(1)} %get-tuple-element.23.g_all) | copy-start | bytes 11010052
  53.8 31.3 %collective-permute-start.2 = (bf16[384,256]{1,0:T(8,128)(2,1)S(1)}, bf16[384,256]{1,0:T(8,128)(2,1)S(1)}, u32[]{:S(2)}, u32[]{:S(2)}) collective-permute-start(bf16[384,256]{1,0:T(8,128)(2,1)S(1)} %get-tuple-element.47), channel_id=1, source_target_pairs={{0,3},{1,0},{2,1},{3,2},{4,7},{5,4},{6,5},{7,6},{8,11},{9,8},{10,9... | collective-permute-start | bytes 589832 | tf_op jit(solution)/shard_map/ppermute | solution.py:297
  56.1 29.0 %collective-permute-start.1 = (bf16[384,256]{1,0:T(8,128)(2,1)S(1)}, bf16[384,256]{1,0:T(8,128)(2,1)S(1)}, u32[]{:S(2)}, u32[]{:S(2)}) collective-permute-start(bf16[384,256]{1,0:T(8,128)(2,1)S(1)} %get-tuple-element.48), channel_id=1, source_target_pairs={{0,2},{1,3},{2,0},{3,1},{4,6},{5,7},{6,4},{7,5},{8,10},{9,11},{10,... | collective-permute-start | bytes 589832 | tf_op jit(solution)/shard_map/ppermute | solution.py:297
  56.1 29.0 %collective-permute-start = (bf16[384,256]{1,0:T(8,128)(2,1)S(1)}, bf16[384,256]{1,0:T(8,128)(2,1)S(1)}, u32[]{:S(2)}, u32[]{:S(2)}) collective-permute-start(bf16[384,256]{1,0:T(8,128)(2,1)S(1)} %get-tuple-element.49), channel_id=1, source_target_pairs={{0,1},{1,2},{2,3},{3,0},{4,5},{5,6},{6,7},{7,4},{8,9},{9,10},{10,1... | collective-permute-start | bytes 589832 | tf_op jit(solution)/shard_map/ppermute | solution.py:297
  85.3 5.9 %collective-permute-start.6 = (bf16[4,384,256]{2,1,0:T(8,128)(2,1)S(1)}, bf16[4,384,256]{2,1,0:T(8,128)(2,1)}, u32[]{:S(2)}, u32[]{:S(2)}) collective-permute-start(bf16[4,384,256]{2,1,0:T(8,128)(2,1)S(1)} %pad_maximum_fusion.s_own), channel_id=1, source_target_pairs={{0,16},{16,0},{1,17},{17,1},{2,18},{18,2},{3,19},{19,3},{4,20},{20... | collective-permute-start | bytes 2359304 | tf_op jit(solution)/shard_map/ppermute | solution.py:316
  85.8 33.9 %collective-permute-start.5 = (bf16[384,256]{1,0:T(8,128)(2,1)S(1)}, bf16[384,256]{1,0:T(8,128)(2,1)S(1)}, u32[]{:S(2)}, u32[]{:S(2)}) collective-permute-start(bf16[384,256]{1,0:T(8,128)(2,1)S(1)} %get-tuple-element.43), channel_id=1, source_target_pairs={{0,1},{1,2},{2,3},{3,0},{4,5},{5,6},{6,7},{7,4},{8,9},{9,10},{10,1... | collective-permute-start | bytes 589832 | tf_op jit(solution)/shard_map/ppermute | solution.py:318
  88.7 31.0 %collective-permute-start.4 = (bf16[384,256]{1,0:T(8,128)(2,1)S(1)}, bf16[384,256]{1,0:T(8,128)(2,1)S(1)}, u32[]{:S(2)}, u32[]{:S(2)}) collective-permute-start(bf16[384,256]{1,0:T(8,128)(2,1)S(1)} %get-tuple-element.44), channel_id=1, source_target_pairs={{0,2},{1,3},{2,0},{3,1},{4,6},{5,7},{6,4},{7,5},{8,10},{9,11},{10,... | collective-permute-start | bytes 589832 | tf_op jit(solution)/shard_map/ppermute | solution.py:318
  89.6 30.1 %collective-permute-start.3 = (bf16[384,256]{1,0:T(8,128)(2,1)S(1)}, bf16[384,256]{1,0:T(8,128)(2,1)S(1)}, u32[]{:S(2)}, u32[]{:S(2)}) collective-permute-start(bf16[384,256]{1,0:T(8,128)(2,1)S(1)} %get-tuple-element.45), channel_id=1, source_target_pairs={{0,3},{1,0},{2,1},{3,2},{4,7},{5,4},{6,5},{7,6},{8,11},{9,8},{10,9... | collective-permute-start | bytes 589832 | tf_op jit(solution)/shard_map/ppermute | solution.py:318
  91.2 2.0 %copy-start.1 = (bf16[4,128,3584]{2,1,0:T(8,128)(2,1)S(1)}, bf16[4,128,3584]{2,1,0:T(8,128)(2,1)}, u32[]{:S(2)}) copy-start(bf16[4,128,3584]{2,1,0:T(8,128)(2,1)} %copy-done) | copy-start | bytes 11010052
  93.2 26.5 %copy-start.4 = (bf16[128,8,256]{2,1,0:T(8,128)(2,1)S(1)}, bf16[128,8,256]{2,1,0:T(8,128)(2,1)}, u32[]{:S(2)}) copy-start(bf16[128,8,256]{2,1,0:T(8,128)(2,1)} %param.8) | copy-start | bytes 1572868
  121.9 5.6 %collective-permute-start.9 = (f32[128,8]{1,0:T(8,128)S(1)}, f32[128,8]{1,0:T(8,128)S(1)}, u32[]{:S(2)}, u32[]{:S(2)}) collective-permute-start(f32[128,8]{1,0:T(8,128)S(1)} %get-tuple-element.41), channel_id=1, source_target_pairs={{0,12},{4,8},{8,4},{12,0},{1,13},{5,9},{9,5},{13,1},{2,14},{6,10},... | collective-permute-start | bytes 12296 | tf_op jit(solution)/shard_map/ppermute | solution.py:333
  123.3 4.7 %collective-permute-start.8 = (f32[128,8]{1,0:T(8,128)S(1)}, f32[128,8]{1,0:T(8,128)S(1)}, u32[]{:S(2)}, u32[]{:S(2)}) collective-permute-start(f32[128,8]{1,0:T(8,128)S(1)} %get-tuple-element.41), channel_id=1, source_target_pairs={{0,8},{4,12},{8,0},{12,4},{1,9},{5,13},{9,1},{13,5},{2,10},{6,14},... | collective-permute-start | bytes 12296 | tf_op jit(solution)/shard_map/ppermute | solution.py:333
  124.1 4.3 %collective-permute-start.7 = (f32[128,8]{1,0:T(8,128)S(1)}, f32[128,8]{1,0:T(8,128)S(1)}, u32[]{:S(2)}, u32[]{:S(2)}) collective-permute-start(f32[128,8]{1,0:T(8,128)S(1)} %get-tuple-element.41), channel_id=1, source_target_pairs={{0,4},{4,0},{8,12},{12,8},{1,5},{5,1},{9,13},{13,9},{2,6},{6,2},{1... | collective-permute-start | bytes 12296 | tf_op jit(solution)/shard_map/ppermute | solution.py:333

commit v3 on v2

--- a/solution.py
+++ b/solution.py
@@ -120,26 +120,39 @@
         ids.append(send(ids_ref, ids_all.at[0, j], i_snd.at[0, j], i_rcv.at[0, j], to_z[j]))
         ids.append(send(ids_ref, ids_all.at[1, j], i_snd.at[1, j], i_rcv.at[1, j], other[j]))
 
-    for j in order:
-        a[j].wait_recv()
-        x[j] = send(shard(j, sec), shard(j, sec), x_snd.at[j], x_rcv.at[j], to_x)
-        y[j] = send(shard(j, sec), shard(j, sec), y_snd.at[j], y_rcv.at[j], to_y)
-    d = {}
-    for j in (0,) + order:
+    d, h = {}, []
+    mate_cols = pl.ds(pl.multiple_of(mate * half, 128), half)
+
+    def relay(j):
         if j % 2 == 0:
             x[j].wait_recv()
             d[j] = send(shard(j, sx), shard(j, sx), d_snd.at[j], d_rcv.at[j], to_y)
         else:
             y[j].wait_recv()
             d[j] = send(shard(j, sy), shard(j, sy), d_snd.at[j], d_rcv.at[j], to_x)
-    for c in own:
-        c.wait()
-    h = []
-    mate_cols = pl.ds(pl.multiple_of(mate * half, 128), half)
-    for j in (0,) + order:
+
+    def pass_half(j):
         (y if j % 2 == 0 else x)[j].wait_recv()
         d[j].wait_recv()
         h.append(send(g_all.at[j, :, mate_cols], g_half.at[j], h_snd.at[j], h_rcv.at[j], to_mate))
+
+    def onward(j):
+        a[j].wait_recv()
+        x[j] = send(shard(j, sec), shard(j, sec), x_snd.at[j], x_rcv.at[j], to_x)
+        y[j] = send(shard(j, sec), shard(j, sec), y_snd.at[j], y_rcv.at[j], to_y)
+
+    relay(0)
+    onward(1)
+    onward(3)
+    relay(1)
+    relay(3)
+    onward(2)
+    for c in own:
+        c.wait()
+    pass_half(0)
+    relay(2)
+    for j in order:
+        pass_half(j)
     for c in ids + h:
         c.wait_recv()
     for c in [*a.values(), *x.values(), *y.values(), *d.values(), *ids, *h]:

time: 130 us -> 131 us (level)
  no operation moved by 1% of the time
where the time goes in v3:
time: 131 us; the launch traced here: 130 us
  Pallas kernels  101 us (77%)
  starting transfers between devices  12.1 us (9%)
  local copies, waits for them, and re-layouts  5.51 us (4%)
  matrix products  5.15 us (4%)
  waiting for transfers between devices  3.21 us (2%)
  other arithmetic  2.27 us (2%)
    pallas_call x1, Pallas kernels, spread_call(): pl.pallas_call(spread, out_shape=shapes, in_specs=[VMEM] * 2, out_specs=(...  46.6 us
    pallas_call x1, Pallas kernels, hidden_call(): pl.pallas_call(functools.partial(hidden_kernel, padded, capacity), grid=(...  27.8 us
    pallas_call x1, Pallas kernels, weight_call(): pl.pallas_call(functools.partial(weight_kernel, padded, capacity), grid=(...  26.5 us
    ppermute x3, starting transfers between devices, local(): lax.ppermute(returning[j], 'expert', [(i, (i - j) % 4) for i in range(4)])  5.3 us
    unnamed x12, local copies, waits for them, and re-layouts  5.12 us
    ppermute x3, starting transfers between devices, local(): lax.ppermute(share, 'section', [(i, i ^ m) for i in range(4)])  3.49 us
    ppermute x3, starting transfers between devices, local(): lax.ppermute(send_scaled[j], 'expert', [(i, (i + j) % 4) for i in range(4)])  3.21 us
    ppermute x3, waiting for transfers between devices, local(): lax.ppermute(share, 'section', [(i, i ^ m) for i in range(4)])  3.2 us
  transfers between devices with their start and end apart: 10, of which 3 were waited for; matrix products, arithmetic and copies ran while one was open for 1% of the time, Pallas kernels for 42%

profile of v3, /device:TPU:0, one launch (start us, length us, event | category | flops | bytes accessed | tf_op | source)
XLA Modules:
  0.0 130.0 jit_solution(8692581929440334724)
XLA Ops:
  0.6 0.7 compare_select_fusion
  1.6 0.7 convert_add_fusion
  2.5 0.8 copy.20
  3.3 0.9 copy-done.2
  4.2 0.7 copy-done.3
  4.9 46.6 %shard_map.76 = (bf16[4,128,3584]{2,1,0:T(8,128)(2,1)S(1)}, bf16[4,128,1792]{2,1,0:T(8,128)(2,1)S(1)}, s32[2,4,8,128]{3,2,1,0:T(8,128)S(1)}) custom-call(bf16[128,896]{1,0:T(8,128)(2,1)S(1)} %copy-done.2, s32[8,128]{1,0:T(8,128)S(1)} %bitcast.41), custom_call_target="tpu_custom_call" | custom-call | tf_op jit(solution)/shard_map/pallas_call | solution.py:172
  51.5 2.8 %fusion.4 = bf16[1536,256]{1,0:T(8,128)(2,1)S(1)} fusion(s32[1024]{0:T(1024)S(1)} %eq.81, bf16[128,8,256]{2,1,0:T(8,128)(2,1)} %param.8, f32[128,8]{1,0:T(8,128)S(1)} %copy.20), kind=kOutput, calls=%fused_computation.6 | convolution fusion | flops 808058880 | bytes 1318912 | tf_op jit(solution)/shard_map/dot_general | solution.py:306
  54.3 2.6 %collective-permute-start.2 = (bf16[384,256]{1,0:T(8,128)(2,1)S(1)}, bf16[384,256]{1,0:T(8,128)(2,1)S(1)}, u32[]{:S(2)}, u32[]{:S(2)}) collective-permute-start(bf16[384,256]{1,0:T(8,128)(2,1)S(1)} %get-tuple-element.47), channel_id=1, source_target_pairs={{0,3},{1,0},{2,1},{3,2},{4,7},{5,4},{6,5},{7,6},{8,11},{9,8},{10,9... | collective-permute-start | bytes 589832 | tf_op jit(solution)/shard_map/ppermute | solution.py:310
  57.0 0.6 collective-permute-start
  58.1 27.8 %shard_map.77 = bf16[4,384,256]{2,1,0:T(8,128)(2,1)S(1)} custom-call(bf16[4,512,128]{2,1,0:T(8,128)(2,1)S(1)} %bitcast.40, bf16[4,128,3584]{2,1,0:T(8,128)(2,1)S(1)} %get-tuple-element.23.g_all, bf16[16,256,3584]{2,1,0:T(8,128)(2,1)} %w_ref.1), custom_call_target="tpu_custom_call" | custom-call | flops 3758096384 | bytes 29360128 | tf_op jit(solution)/shard_map/pallas_call | solution.py:228
  86.2 0.3 fusion.5.pick
  86.6 2.9 %collective-permute-start.5 = (bf16[384,256]{1,0:T(8,128)(2,1)S(1)}, bf16[384,256]{1,0:T(8,128)(2,1)S(1)}, u32[]{:S(2)}, u32[]{:S(2)}) collective-permute-start(bf16[384,256]{1,0:T(8,128)(2,1)S(1)} %get-tuple-element.43), channel_id=1, source_target_pairs={{0,1},{1,2},{2,3},{3,0},{4,5},{5,6},{6,7},{7,4},{8,9},{9,10},{10,1... | collective-permute-start | bytes 589832 | tf_op jit(solution)/shard_map/ppermute | solution.py:331
  89.5 1.0 collective-permute-start.4
  90.5 1.4 %collective-permute-start.3 = (bf16[384,256]{1,0:T(8,128)(2,1)S(1)}, bf16[384,256]{1,0:T(8,128)(2,1)S(1)}, u32[]{:S(2)}, u32[]{:S(2)}) collective-permute-start(bf16[384,256]{1,0:T(8,128)(2,1)S(1)} %get-tuple-element.45), channel_id=1, source_target_pairs={{0,3},{1,0},{2,1},{3,2},{4,7},{5,4},{6,5},{7,6},{8,11},{9,8},{10,9... | collective-permute-start | bytes 589832 | tf_op jit(solution)/shard_map/ppermute | solution.py:331
  91.9 2.0 %copy-done.1 = bf16[4,128,3584]{2,1,0:T(8,128)(2,1)S(1)} copy-done((bf16[4,128,3584]{2,1,0:T(8,128)(2,1)S(1)}, bf16[4,128,3584]{2,1,0:T(8,128)(2,1)}, u32[]{:S(2)}) %copy-start.1) | copy-done | bytes 3670040
  93.9 26.5 %shard_map.78 = bf16[16,256,1792]{2,1,0:T(8,128)(2,1)} custom-call(s32[1]{0:T(128)} %bitcast.14.dp_ref, bf16[2,4,512,128]{3,2,1,0:T(8,128)(2,1)S(1)} %fusion.5.pick, bf16[4,128,3584]{2,1,0:T(8,128)(2,1)S(1)} %copy-done.1, bf16[4,128,1792]{2,1,0:T(8,128)(2,1)S(1)} %get-tuple-element.25.g_half, bf16[4,384,256]{2,1,0:T(8,128)(2,1)S(1)} %pad_maximum_fusion.s_own, ...), custom_call_target="tpu_custom_call" | custom-call | flops 3758096384 | bytes 14680064 | tf_op jit(solution)/shard_map/pallas_call | solution.py:270
  120.5 2.1 %fusion.9 = (f32[128,8]{1,0:T(8,128)S(1)}, bf16[128,8,256]{2,1,0:T(8,128)(2,1)}) fusion(bf16[128,8,256]{2,1,0:T(8,128)(2,1)S(1)} %copy-done.4, f32[128,8]{1,0:T(8,128)S(1)} %copy.20, bf16[384,256]{1,0:T(8,128)(2,1)S(1)} %collective-permute-done.5, bf16[384,256]{1,0:T(8,128)(2,1)S(1)} %collective-permute-done.4, ...), kind=kOutput, calls=%fused_computation.15 | convolution fusion | flops 811334656 | bytes 1847296 | tf_op jit(solution)/shard_map/dot_general | solution.py:342
  122.6 1.9 %collective-permute-start.9 = (f32[128,8]{1,0:T(8,128)S(1)}, f32[128,8]{1,0:T(8,128)S(1)}, u32[]{:S(2)}, u32[]{:S(2)}) collective-permute-start(f32[128,8]{1,0:T(8,128)S(1)} %get-tuple-element.41), channel_id=1, source_target_pairs={{0,12},{4,8},{8,4},{12,0},{1,13},{5,9},{9,5},{13,1},{2,14},{6,10},... | collective-permute-start | bytes 12296 | tf_op jit(solution)/shard_map/ppermute | solution.py:346
  124.5 0.5 collective-permute-start.8
  125.0 1.1 collective-permute-start.7
  126.1 1.9 %collective-permute-done.9 = f32[128,8]{1,0:T(8,128)S(1)} collective-permute-done((f32[128,8]{1,0:T(8,128)S(1)}, f32[128,8]{1,0:T(8,128)S(1)}, u32[]{:S(2)}, u32[]{:S(2)}) %collective-permute-start.9) | collective-permute-done | bytes 4128 | tf_op jit(solution)/shard_map/ppermute | solution.py:346
  128.0 0.8 collective-permute-done.8
  128.8 0.5 collective-permute-done.7
  129.3 0.7 copy.22
  (32 shorter events, 1.4 us)
Async XLA Ops:
  3.3 0.9 copy-start.2
  4.2 0.7 copy-start.3
  51.5 6.6 %copy-start = (bf16[4,128,3584]{2,1,0:T(8,128)(2,1)}, bf16[4,128,3584]{2,1,0:T(8,128)(2,1)S(1)}, u32[]{:S(2)}) copy-start(bf16[4,128,3584]{2,1,0:T(8,128)(2,1)S(1)} %get-tuple-element.23.g_all) | copy-start | bytes 11010052
  54.3 31.6 %collective-permute-start.2 = (bf16[384,256]{1,0:T(8,128)(2,1)S(1)}, bf16[384,256]{1,0:T(8,128)(2,1)S(1)}, u32[]{:S(2)}, u32[]{:S(2)}) collective-permute-start(bf16[384,256]{1,0:T(8,128)(2,1)S(1)} %get-tuple-element.47), channel_id=1, source_target_pairs={{0,3},{1,0},{2,1},{3,2},{4,7},{5,4},{6,5},{7,6},{8,11},{9,8},{10,9... | collective-permute-start | bytes 589832 | tf_op jit(solution)/shard_map/ppermute | solution.py:310
  56.9 29.1 %collective-permute-start.1 = (bf16[384,256]{1,0:T(8,128)(2,1)S(1)}, bf16[384,256]{1,0:T(8,128)(2,1)S(1)}, u32[]{:S(2)}, u32[]{:S(2)}) collective-permute-start(bf16[384,256]{1,0:T(8,128)(2,1)S(1)} %get-tuple-element.48), channel_id=1, source_target_pairs={{0,2},{1,3},{2,0},{3,1},{4,6},{5,7},{6,4},{7,5},{8,10},{9,11},{10,... | collective-permute-start | bytes 589832 | tf_op jit(solution)/shard_map/ppermute | solution.py:310
  57.0 29.0 %collective-permute-start = (bf16[384,256]{1,0:T(8,128)(2,1)S(1)}, bf16[384,256]{1,0:T(8,128)(2,1)S(1)}, u32[]{:S(2)}, u32[]{:S(2)}) collective-permute-start(bf16[384,256]{1,0:T(8,128)(2,1)S(1)} %get-tuple-element.49), channel_id=1, source_target_pairs={{0,1},{1,2},{2,3},{3,0},{4,5},{5,6},{6,7},{7,4},{8,9},{9,10},{10,1... | collective-permute-start | bytes 589832 | tf_op jit(solution)/shard_map/ppermute | solution.py:310
  86.1 5.8 %collective-permute-start.6 = (bf16[4,384,256]{2,1,0:T(8,128)(2,1)S(1)}, bf16[4,384,256]{2,1,0:T(8,128)(2,1)}, u32[]{:S(2)}, u32[]{:S(2)}) collective-permute-start(bf16[4,384,256]{2,1,0:T(8,128)(2,1)S(1)} %pad_maximum_fusion.s_own), channel_id=1, source_target_pairs={{0,16},{16,0},{1,17},{17,1},{2,18},{18,2},{3,19},{19,3},{4,20},{20... | collective-permute-start | bytes 2359304 | tf_op jit(solution)/shard_map/ppermute | solution.py:329
  86.6 33.9 %collective-permute-start.5 = (bf16[384,256]{1,0:T(8,128)(2,1)S(1)}, bf16[384,256]{1,0:T(8,128)(2,1)S(1)}, u32[]{:S(2)}, u32[]{:S(2)}) collective-permute-start(bf16[384,256]{1,0:T(8,128)(2,1)S(1)} %get-tuple-element.43), channel_id=1, source_target_pairs={{0,1},{1,2},{2,3},{3,0},{4,5},{5,6},{6,7},{7,4},{8,9},{9,10},{10,1... | collective-permute-start | bytes 589832 | tf_op jit(solution)/shard_map/ppermute | solution.py:331
  89.5 31.0 %collective-permute-start.4 = (bf16[384,256]{1,0:T(8,128)(2,1)S(1)}, bf16[384,256]{1,0:T(8,128)(2,1)S(1)}, u32[]{:S(2)}, u32[]{:S(2)}) collective-permute-start(bf16[384,256]{1,0:T(8,128)(2,1)S(1)} %get-tuple-element.44), channel_id=1, source_target_pairs={{0,2},{1,3},{2,0},{3,1},{4,6},{5,7},{6,4},{7,5},{8,10},{9,11},{10,... | collective-permute-start | bytes 589832 | tf_op jit(solution)/shard_map/ppermute | solution.py:331
  90.5 30.0 %collective-permute-start.3 = (bf16[384,256]{1,0:T(8,128)(2,1)S(1)}, bf16[384,256]{1,0:T(8,128)(2,1)S(1)}, u32[]{:S(2)}, u32[]{:S(2)}) collective-permute-start(bf16[384,256]{1,0:T(8,128)(2,1)S(1)} %get-tuple-element.45), channel_id=1, source_target_pairs={{0,3},{1,0},{2,1},{3,2},{4,7},{5,4},{6,5},{7,6},{8,11},{9,8},{10,9... | collective-permute-start | bytes 589832 | tf_op jit(solution)/shard_map/ppermute | solution.py:331
  91.9 2.0 %copy-start.1 = (bf16[4,128,3584]{2,1,0:T(8,128)(2,1)S(1)}, bf16[4,128,3584]{2,1,0:T(8,128)(2,1)}, u32[]{:S(2)}) copy-start(bf16[4,128,3584]{2,1,0:T(8,128)(2,1)} %copy-done) | copy-start | bytes 11010052
  93.9 26.5 %copy-start.4 = (bf16[128,8,256]{2,1,0:T(8,128)(2,1)S(1)}, bf16[128,8,256]{2,1,0:T(8,128)(2,1)}, u32[]{:S(2)}) copy-start(bf16[128,8,256]{2,1,0:T(8,128)(2,1)} %param.8) | copy-start | bytes 1572868
  122.6 5.4 %collective-permute-start.9 = (f32[128,8]{1,0:T(8,128)S(1)}, f32[128,8]{1,0:T(8,128)S(1)}, u32[]{:S(2)}, u32[]{:S(2)}) collective-permute-start(f32[128,8]{1,0:T(8,128)S(1)} %get-tuple-element.41), channel_id=1, source_target_pairs={{0,12},{4,8},{8,4},{12,0},{1,13},{5,9},{9,5},{13,1},{2,14},{6,10},... | collective-permute-start | bytes 12296 | tf_op jit(solution)/shard_map/ppermute | solution.py:346
  124.5 4.3 %collective-permute-start.8 = (f32[128,8]{1,0:T(8,128)S(1)}, f32[128,8]{1,0:T(8,128)S(1)}, u32[]{:S(2)}, u32[]{:S(2)}) collective-permute-start(f32[128,8]{1,0:T(8,128)S(1)} %get-tuple-element.41), channel_id=1, source_target_pairs={{0,8},{4,12},{8,0},{12,4},{1,9},{5,13},{9,1},{13,5},{2,10},{6,14},... | collective-permute-start | bytes 12296 | tf_op jit(solution)/shard_map/ppermute | solution.py:346
  125.0 4.3 %collective-permute-start.7 = (f32[128,8]{1,0:T(8,128)S(1)}, f32[128,8]{1,0:T(8,128)S(1)}, u32[]{:S(2)}, u32[]{:S(2)}) collective-permute-start(f32[128,8]{1,0:T(8,128)S(1)} %get-tuple-element.41), channel_id=1, source_target_pairs={{0,4},{4,0},{8,12},{12,8},{1,5},{5,1},{9,13},{13,9},{2,6},{6,2},{1... | collective-permute-start | bytes 12296 | tf_op jit(solution)/shard_map/ppermute | solution.py:346
